TPU v7x, 32 devices: a whole 2x2x4 slice. The times are simulated.
32 devices in a mesh: parts: 2 (over y), row: 4 (over z), col: 4 (over x, core).
Axes of the slice: x: 2, y: 2, z: 4, core: 2. Of those that a mesh axis runs over, the one named last changes fastest.
Arguments:
- amplitudes: bfloat16 [8, 100, 512, 512], P('parts', 'col', 'row'), parts along dimension 0, may hold values from -12 to 12
- integrals: bfloat16 [200, 512, 512], P(('parts', 'col'), 'row'), parts along dimension 0, may hold values from -0.109375 to 0.109375
- occ_irrep: int32 [200], P('parts'), parts along dimension 0, may hold values from 0 to 7, as said below
- vir_irrep: int32 [1024], P('parts'), parts along dimension 0, may hold values from 0 to 7, as said below
- screen: int32 [200, 8], P('parts'), parts along dimension 0, may hold values 0 or 1
- occ_energy: float32 [200], P('parts'), parts along dimension 0, may hold values from -1 to -0.3
- vir_energy: float32 [1024], P('parts'), parts along dimension 0, may hold values from 0.1 to 1
Outputs:
- update: float32 [512, 8, 512], P('row', 'parts', 'col'), parts along dimension 1
There are 2 independent parts, one for each index of `parts`. A program takes and returns all parts, laid end to end along the dimension named above; each array names one. Nothing has to cross between parts.
Inputs may be any that keep to these rules, and one draw needn't show every extreme that they name: `occ_irrep`: the labels never fall from one orbital to the next; the first is 0 and the last is 7. `vir_irrep`: the labels never fall from one orbital to the next and every label from 0 to 7 occurs; exactly one label covers 256 virtual orbitals, every other label fewer.
All inputs are finite; a program needn't handle non-finite values.
Results may differ from a plain program's by a relative error of at most 0.0003.
Values may be sent and summed in bfloat16 or wider, within the bound.
No kernel may reach another device: no remote copies, remote signals or barrier semaphores. Data moves between devices by JAX's collectives and lax.ppermute only.
A program may use at most 128 MiB of HBM per device.

v0:
```python
import jax
import jax.numpy as jnp
from jax import lax
from jax.experimental import pallas as pl
from jax.experimental.pallas import tpu as pltpu
from jax.sharding import PartitionSpec as P

FOLD = 256
K_STEP = 5


def folded_integrals(integrals, occ_local, vir_local, vir_irrep, pair_label, screen_rows):
    irrep_codes = jnp.arange(8, dtype=jnp.int32)
    screen_local = jnp.sum(
        screen_rows[:, None, :] * (vir_local[None, :, None] == irrep_codes).astype(jnp.int32),
        axis=2,
    )
    target = jnp.bitwise_xor(
        jnp.bitwise_xor(occ_local[:, None], vir_local[None, :]), pair_label
    )
    target = jnp.where(screen_local == 1, target, -1)
    keep = target[:, :, None] == vir_irrep[None, None, :]
    kept = jnp.where(keep, integrals, jnp.zeros_like(integrals))
    return kept[:, :, :FOLD] + kept[:, :, FOLD:]


NARROW = 64
CAPS = (22, 3)
FEW_CAPS = (4, 10)
FEW_WIDE = 7


def largest_irrep(vir_ref):
    return jnp.where(vir_ref[0] == vir_ref[FOLD - 1], vir_ref[0], vir_ref[FOLD])


def label_columns(row_labels):
    return jnp.transpose(jnp.broadcast_to(row_labels, (8, row_labels.shape[1])))


def as_bf16(labels):
    return labels.astype(jnp.float32).astype(jnp.bfloat16)


def label_mix(mix_ref, column_ref, row_ref, row, big, keep_big):
    depth = mix_ref.shape[0]
    column_ref[...] = label_columns(row_ref[...])
    column = column_ref[pl.ds(pl.multiple_of(row * depth, depth), depth), :1]
    is_big = row_ref[...] == big
    wanted = is_big if keep_big else jnp.logical_not(is_big)
    mix_ref[...] = as_bf16(jnp.where(wanted, jnp.bitwise_xor(column, row_ref[...]), 8))


def kept_folded(int_ref, mix_ref, j, x):
    tile = int_ref[j]
    wanted = as_bf16(jnp.full(mix_ref.shape, x))
    kept = jnp.where(mix_ref[...] == wanted, tile, jnp.zeros_like(tile))
    return kept[:, :FOLD] + kept[:, FOLD:]


def narrow_fold(kept, bits, local):
    half = kept.shape[0] // 2
    lane = lax.broadcasted_iota(jnp.int32, (half, 2 * NARROW), 1)
    narrow = (kept[:, : 2 * NARROW] + kept[:, 2 * NARROW:]).astype(jnp.float32)
    narrow = narrow + pltpu.roll(narrow, NARROW, 1)
    on = jnp.bitwise_and(lax.shift_right_logical(jnp.full(local.shape, bits), local), 1) == 1
    narrow = jnp.where(on, narrow, 0.0)
    return jnp.where(lane < NARROW, narrow[:half], narrow[half:]).astype(jnp.bfloat16)


def screen_bits(screen_ref, k):
    bits = screen_ref[0, k]
    for g in range(1, 8):
        bits = bits + screen_ref[g, k] * (1 << g)
    return bits


def copy_of(source_ref, int_ref, sems, group):
    here = pl.ds(group * K_STEP, K_STEP)
    return pltpu.make_async_copy(source_ref.at[here], int_ref.at[here], sems.at[group])


def start_copies(source_ref, int_ref, sems):
    for group in range(int_ref.shape[0] // K_STEP):
        copy_of(source_ref, int_ref, sems, group).start()


def wait_copy(source_ref, int_ref, sems, group):
    copy_of(source_ref, int_ref, sems, group).wait()


def wide_kernel(
    occ_ref, vir_ref, screen_ref, place_ref, source_ref, row_ref,
    few_ref, m2a_ref, m2b_ref, m3a_ref, m3b_ref, pos2_ref, pos3_ref, posx_ref, form_ref, count_ref,
    mix_ref, small_mix_ref, column_ref, counts_ref, int_ref, sems, batch,
):
    start_copies(source_ref, int_ref, sems)
    k_all, depth, total = int_ref.shape
    half = depth // 2
    row, col = place_ref[0], place_ref[1]
    pair_label = occ_ref[batch]
    big = largest_irrep(vir_ref)
    mostly_zero = (occ_ref[col * k_all] == pair_label) | (occ_ref[(col + 1) * k_all - 1] == pair_label)
    most = FEW_CAPS[-1]
    for n in range(3):
        counts_ref[n] = 0
    label_mix(mix_ref, column_ref, row_ref, row, big, True)

    @pl.when(mostly_zero)
    def _():
        label_mix(small_mix_ref, column_ref, row_ref, row, big, False)

    local = column_ref[pl.ds(pl.multiple_of(row * depth, depth), depth), :1]

    @pl.loop(0, k_all)
    def _(k):
        @pl.when(k % K_STEP == 0)
        def _():
            wait_copy(source_ref, int_ref, sems, k // K_STEP)

        k_whole = col * k_all + k
        x = jnp.bitwise_xor(occ_ref[k_whole], pair_label)
        on_big = screen_ref[jnp.bitwise_xor(big, x), k_whole] == 1
        actives = (on_big & (x != 0), on_big & (x == 0), x != 0)
        pos2, pos3, posx = [jnp.where(active, counts_ref[n], -1) for n, active in enumerate(actives)]
        for n, active in enumerate(actives):
            counts_ref[n] = counts_ref[n] + active.astype(jnp.int32)
        pos2_ref[k], pos3_ref[k], posx_ref[k] = pos2, pos3, posx

        @pl.when(pos2 >= 0)
        def _():
            wide = kept_folded(int_ref, mix_ref, k, x)
            short = wide[:half] + wide[half:]

            @pl.when(mostly_zero & (posx < most))
            def _():
                for piece in range(2):
                    few_ref[posx, 1 + piece] = short[:, piece * 2 * NARROW:(piece + 1) * 2 * NARROW]

            @pl.when(pos2 < CAPS[0])
            def _():
                m2a_ref[pos2] = short

            @pl.when(pos2 >= CAPS[0])
            def _():
                m2b_ref[pos2 - CAPS[0]] = short

        @pl.when(mostly_zero & (posx >= 0) & (posx < most))
        def _():
            kept = kept_folded(int_ref, small_mix_ref, k, x)
            few_ref[posx, 0] = narrow_fold(kept, screen_bits(screen_ref, k_whole), local)

            @pl.when(pos2 < 0)
            def _():
                for piece in range(2):
                    few_ref[posx, 1 + piece] = jnp.zeros((half, 2 * NARROW), jnp.bfloat16)

        @pl.when(pos3 >= 0)
        def _():
            wide = kept_folded(int_ref, mix_ref, k, x)

            @pl.when(pos3 < CAPS[0])
            def _():
                m3a_ref[pos3] = wide

            @pl.when(pos3 >= CAPS[0])
            def _():
                m3b_ref[pos3 - CAPS[0]] = wide

    labels = row_ref[...]
    lanes = lax.broadcasted_iota(jnp.int32, labels.shape, 1)
    ahead = pltpu.roll(labels, total - NARROW, 1)
    long = (labels == ahead) & (lanes < total - NARROW) & (labels != big)
    too_long = jnp.max(long.astype(jnp.int32)) == 1
    n2, n3, nx = counts_ref[0], counts_ref[1], counts_ref[2]
    count_ref[0] = nx
    one_label = occ_ref[0] == pair_label
    form = jnp.where(nx <= FEW_CAPS[0], 3, jnp.where(nx <= FEW_CAPS[1], 4, 5))
    form = jnp.where(mostly_zero & (n3 <= CAPS[0]), form, 5)
    form = jnp.where((n3 <= FEW_WIDE) & (n2 <= CAPS[0]), 2, form)
    form = jnp.where(one_label, form, 6)
    form = jnp.where(n3 == 0, jnp.where(n2 <= CAPS[0], 0, 1), form)
    form_ref[0] = jnp.where(too_long, 6, form)


def wide_blocks(integrals, occ_irrep, vir_irrep, screen, place, batch):
    occ_share, depth, total = integrals.shape
    shapes = [(n, depth // 2, FOLD) for n in CAPS] + [(n, depth, FOLD) for n in CAPS]
    few = (FEW_CAPS[-1], 3, depth // 2, 2 * NARROW)
    smem = pl.BlockSpec(memory_space=pltpu.SMEM)

    def kernel(*refs):
        wide_kernel(*refs, batch)

    vmem = pl.BlockSpec(memory_space=pltpu.VMEM)
    return pl.pallas_call(
        kernel,
        in_specs=[smem] * 4 + [pl.BlockSpec(memory_space=pltpu.HBM), vmem],
        out_specs=[vmem] * (1 + len(shapes)) + [smem] * 5,
        scratch_shapes=[
            pltpu.VMEM((depth, total), jnp.bfloat16),
            pltpu.VMEM((depth, total), jnp.bfloat16),
            pltpu.VMEM((total, 8), jnp.int32),
            pltpu.SMEM((3,), jnp.int32),
            pltpu.VMEM(integrals.shape, jnp.bfloat16),
            pltpu.SemaphoreType.DMA((occ_share // K_STEP,)),
        ],
        out_shape=[jax.ShapeDtypeStruct(v, jnp.bfloat16) for v in [few] + shapes]
        + [jax.ShapeDtypeStruct((n,), jnp.int32) for n in (occ_share, occ_share, occ_share, 1, 1)],
        cost_estimate=cost(5),
        compiler_params=pltpu.CompilerParams(vmem_limit_bytes=24 * 1024 * 1024),
    )(occ_irrep, vir_irrep, screen.T, place, integrals, vir_irrep[None, :])


def narrow_kernel(
    occ_ref, vir_ref, screen_ref, place_ref, source_ref, row_ref, few_ref, narrow_ref,
    mix_ref, column_ref, int_ref, sems, batch,
):
    start_copies(source_ref, int_ref, sems)
    k_all, depth, total = int_ref.shape
    row, col = place_ref[0], place_ref[1]
    label_mix(mix_ref, column_ref, row_ref, row, largest_irrep(vir_ref), False)
    if few_ref is not None:
        for n in range(few_ref.shape[0]):
            for piece in range(2):
                narrow_ref[k_all + 2 * n + piece] = few_ref[n, 1 + piece]
    local = column_ref[pl.ds(pl.multiple_of(row * depth, depth), depth), :1]

    @pl.loop(0, k_all // K_STEP)
    def _(group):
        wait_copy(source_ref, int_ref, sems, group)
        for j in range(K_STEP):
            k = group * K_STEP + j
            k_whole = col * k_all + k
            x = jnp.bitwise_xor(occ_ref[k_whole], occ_ref[batch])
            kept = kept_folded(int_ref, mix_ref, k, x)
            narrow_ref[k] = narrow_fold(kept, screen_bits(screen_ref, k_whole), local)


def narrow_blocks(integrals, occ_irrep, vir_irrep, screen, place, few, batch):
    occ_share, depth, total = integrals.shape
    extra = [] if few is None else [few]
    count = occ_share + sum(2 * v.shape[0] for v in extra)
    smem = pl.BlockSpec(memory_space=pltpu.SMEM)
    vmem = pl.BlockSpec(memory_space=pltpu.VMEM)

    def kernel(*refs):
        narrow_kernel(*(refs if extra else refs[:6] + (None,) + refs[6:]), batch)

    return pl.pallas_call(
        kernel,
        in_specs=[smem] * 4 + [pl.BlockSpec(memory_space=pltpu.HBM), vmem] + [vmem] * len(extra),
        out_specs=vmem,
        out_shape=jax.ShapeDtypeStruct((count, depth // 2, 2 * NARROW), jnp.bfloat16),
        scratch_shapes=[
            pltpu.VMEM((depth, total), jnp.bfloat16),
            pltpu.VMEM((total, 8), jnp.int32),
            pltpu.VMEM(integrals.shape, jnp.bfloat16),
            pltpu.SemaphoreType.DMA((occ_share // K_STEP,)),
        ],
        cost_estimate=cost(4),
        compiler_params=pltpu.CompilerParams(vmem_limit_bytes=16 * 1024 * 1024),
    )(occ_irrep, vir_irrep, screen.T, place, integrals, vir_irrep[None, :], *extra)


def cost(micros):
    return pl.CostEstimate(flops=int(micros * 1e9), bytes_accessed=int(micros * 3e6), transcendentals=0)


SLOTS = (0, 1, 3, 2)
NEAR = 2


def amplitude_rows(column_ref, row_ref, occ_ref, row, batch, share):
    column_ref[...] = label_columns(row_ref[...])
    column = column_ref[pl.ds(pl.multiple_of(row * share, share), share), :1]
    return jnp.concatenate([jnp.bitwise_xor(column, occ_ref[i]) for i in range(batch)], axis=0)


def write_quarters(total_ref, col, outs):
    rows, fold = total_ref.shape
    width, height = fold // 2, rows // 2
    for t, out_ref in enumerate(outs):
        goal = jnp.bitwise_xor(col, t)
        lanes = pl.ds(pl.multiple_of((goal % 2) * width, width), width)
        lines = pl.ds(pl.multiple_of((goal // 2) * height, height), height)
        out_ref[...] = total_ref[lines, lanes].reshape(out_ref.shape)


def chosen(refs, starts, pos, pick):
    block = None
    for n, group in enumerate(refs):
        inside = (pos >= starts[n]) & (pos < starts[n + 1])
        at = jnp.clip(pos - starts[n], 0, starts[n + 1] - starts[n] - 1)
        found = pick(group, at)
        found = jnp.where(inside, found, jnp.zeros_like(found))
        block = found if block is None else block + found
    return block


def starts_of(arrays):
    starts = [0]
    for v in arrays:
        starts.append(starts[-1] + v.shape[0])
    return starts


def mask_kernel(
    occ_ref, place_ref, posx_ref, amp_ref, row_ref, lhs_ref, third_ref, far_ref, fold_ref, few_lhs_ref,
    mix_ref, column_ref, amp_buffer, sems,
):
    batch, k_all, share, total = amp_ref.shape
    rows, groups = batch * share, k_all // K_STEP
    row, col = place_ref[0], place_ref[1]

    def fetch(group):
        slot = group % 2
        source = amp_ref.at[:, pl.ds(group * K_STEP, K_STEP)]
        return pltpu.make_async_copy(source, amp_buffer.at[slot], sems.at[slot])

    fetch(0).start()
    column = amplitude_rows(column_ref, row_ref, occ_ref, row, batch, share)
    mix_ref[...] = as_bf16(jnp.bitwise_xor(column, row_ref[...]))
    if few_lhs_ref is not None:
        few_lhs_ref[...] = jnp.zeros(few_lhs_ref.shape, jnp.bfloat16)

    @pl.loop(0, groups)
    def _(group):
        slot = group % 2

        @pl.when(group + 1 < groups)
        def _():
            fetch(group + 1).start()

        fetch(group).wait()

        @pl.loop(0, K_STEP)
        def _(j):
            wanted = as_bf16(jnp.full((rows, share), occ_ref[col * k_all + group * K_STEP + j]))
            folded = None
            for n, s in enumerate(SLOTS):
                place = pl.ds(pl.multiple_of(jnp.bitwise_xor(row, s) * share, share), share)
                tile = amp_buffer[slot, :, j, :, place].reshape(rows, share)
                piece = jnp.where(mix_ref[:, place] == wanted, tile, jnp.zeros_like(tile))
                if n < NEAR:
                    lhs_ref[group, :, pl.ds(pl.multiple_of((n * K_STEP + j) * share, share), share)] = piece
                else:
                    own_ref = third_ref if n == NEAR else far_ref
                    own_ref[group, :, pl.ds(pl.multiple_of(j * share, share), share)] = piece
                folded = piece if folded is None else folded + piece
            if fold_ref is not None:
                fold_ref[group, :, pl.ds(pl.multiple_of(j * share, share), share)] = folded
            else:
                posx = posx_ref[group * K_STEP + j]

                @pl.when((posx >= 0) & (posx < few_lhs_ref.shape[2] // share))
                def _():
                    here = pl.ds(pl.multiple_of(j * share, share), share)
                    there = pl.ds(pl.multiple_of(posx * share, share), share)
                    few_lhs_ref[0, :, there] = third_ref[group, :, here]
                    few_lhs_ref[1, :, there] = far_ref[group, :, here]
                    few_lhs_ref[2, :, there] = folded


def masked_amplitudes(amplitudes, occ_irrep, vir_irrep, place, posx, few):
    batch, k_all, share, total = amplitudes.shape
    rows, groups = batch * share, k_all // K_STEP
    smem = pl.BlockSpec(memory_space=pltpu.SMEM)
    vmem = pl.BlockSpec(memory_space=pltpu.VMEM)
    hbm = pl.BlockSpec(memory_space=pltpu.HBM)
    shapes = [(groups, rows, w) for w in (NEAR * K_STEP * share, K_STEP * share, K_STEP * share)]
    shapes += [(3, rows, few * share)] if few else [(groups, rows, K_STEP * share)]

    def kernel(*refs):
        mask_kernel(*(refs[:8] + (None,) + refs[8:] if few else refs[:9] + (None,) + refs[9:]))

    return pl.pallas_call(
        kernel,
        in_specs=[smem, smem, smem, hbm, vmem],
        out_specs=[vmem] * len(shapes),
        out_shape=[jax.ShapeDtypeStruct(v, jnp.bfloat16) for v in shapes],
        scratch_shapes=[
            pltpu.VMEM((rows, total), jnp.bfloat16),
            pltpu.VMEM((total, 8), jnp.int32),
            pltpu.VMEM((2, batch, K_STEP, share, total), jnp.bfloat16),
            pltpu.SemaphoreType.DMA((2,)),
        ],
        cost_estimate=cost(7),
        compiler_params=pltpu.CompilerParams(vmem_limit_bytes=28 * 1024 * 1024),
    )(occ_irrep, place, posx, amplitudes, vir_irrep[None, :])


def make_first_kernel(few, n3, starts3):
    def kernel(pos3_ref, place_ref, lhs_ref, third_ref, far_ref, *refs):
        sources = 3 if few else 5
        narrow_refs, refs = refs[:sources], refs[sources:]
        m3_refs = [refs[3 * n:3 * n + 3] for n in range(n3)]
        narrow_sum, wide_sum, narrow_rhs, wide_rhs = refs[3 * n3:]
        row = place_ref[0]
        at_end = (row == 0) | (row == 3)
        groups, _, depth = lhs_ref.shape
        share = depth // (NEAR * K_STEP)
        half = share // 2
        lane = lax.broadcasted_iota(jnp.int32, (half, 2 * NARROW), 1)

        narrow_sum[...] = jnp.zeros(narrow_sum.shape, jnp.float32)
        wide_sum[...] = jnp.zeros(wide_sum.shape, jnp.float32)

        @pl.loop(0, groups)
        def _(group):
            @pl.loop(0, K_STEP)
            def _(j):
                k = group * K_STEP + j
                if few:
                    blocks = [ref[k] for ref in narrow_refs]
                else:
                    own, e1, o1, e2, o2 = [ref[k] for ref in narrow_refs]
                    blocks = (own, e1, o1, jnp.where(at_end, e2, o2))
                for n, block in enumerate(blocks):
                    zero = jnp.zeros_like(block)
                    first = pl.multiple_of((n * K_STEP + j) * share, share)
                    narrow_rhs[pl.ds(first, half)] = jnp.where(lane < NARROW, block, zero)
                    narrow_rhs[pl.ds(first + half, half)] = jnp.where(lane < NARROW, zero, block)
                for n in range(3 if n3 else 0):
                    block = chosen(m3_refs, starts3, pos3_ref[k], lambda group, at, n=n: group[n][at])
                    if n == 2:
                        block = jnp.where(at_end, jnp.zeros_like(block), block)
                    wide_rhs[pl.ds(pl.multiple_of((n * K_STEP + j) * share, share), share)] = block

            one = depth // NEAR
            narrow = jnp.dot(lhs_ref[group], narrow_rhs[:depth], preferred_element_type=jnp.float32)
            narrow += jnp.dot(third_ref[group], narrow_rhs[depth:depth + one], preferred_element_type=jnp.float32)
            if not few:
                narrow += jnp.dot(far_ref[group], narrow_rhs[depth + one:], preferred_element_type=jnp.float32)
            narrow_sum[...] += narrow
            if n3:
                wide = jnp.dot(lhs_ref[group], wide_rhs[:depth], preferred_element_type=jnp.float32)
                wide += jnp.dot(third_ref[group], wide_rhs[depth:], preferred_element_type=jnp.float32)
                wide_sum[...] += wide

    return kernel


def first_product(lhs, third_lhs, far_lhs, pos3, place, narrow, few, m3):
    groups, rows, depth = lhs.shape
    vmem = pl.BlockSpec(memory_space=pltpu.VMEM)
    smem = pl.BlockSpec(memory_space=pltpu.SMEM)
    arrays = list(narrow) + [v for group in m3 for v in group]
    wide = (rows, FOLD) if m3 else (16, FOLD)
    wide_depth = depth // NEAR * 3 if m3 else 16
    return pl.pallas_call(
        make_first_kernel(few, len(m3), starts_of([v[0] for v in m3])),
        in_specs=[smem] * 2 + [vmem] * (3 + len(arrays)),
        out_specs=[vmem] * 2,
        out_shape=[jax.ShapeDtypeStruct(v, jnp.float32) for v in ((rows, 2 * NARROW), wide)],
        scratch_shapes=[
            pltpu.VMEM((depth // NEAR * len(SLOTS), 2 * NARROW), jnp.bfloat16),
            pltpu.VMEM((wide_depth, FOLD), jnp.bfloat16),
        ],
        cost_estimate=cost(9 if m3 else 6),
        compiler_params=pltpu.CompilerParams(vmem_limit_bytes=32 * 1024 * 1024),
    )(pos3, place, lhs, third_lhs, far_lhs, *arrays)


def make_last_kernel(few, n2, starts2, n3, starts3):
    def kernel(
        occ_ref, vir_ref, pos2_ref, pos3_ref, count_ref, place_ref, fold_ref, third_ref, far_ref, row_ref, narrow_ref, wide_ref,
        *refs,
    ):
        m2_refs, refs = refs[:n2], refs[n2:]
        m3_refs = [refs[2 * n:2 * n + 2] for n in range(n3)]
        refs = refs[2 * n3:]
        e3_ref, refs = (None, refs) if few else (refs[0], refs[1:])
        outs = refs[:4]
        column_ref, total_ref, narrow_sum, short_rhs, far_rhs, third_rhs = refs[4:]
        row, col = place_ref[0], place_ref[1]
        at_end = (row == 0) | (row == 3)
        groups, rows, width = far_ref.shape if few else fold_ref.shape
        share = width // K_STEP
        batch = rows // share
        @pl.loop(0, groups * K_STEP)
        def _(k):
            here = pl.ds(pl.multiple_of(k * share, share), share)
            if not few:
                short = chosen(m2_refs, starts2, pos2_ref[k], lambda ref, at: ref[at])
                short_rhs[here] = jnp.concatenate([short, short], axis=0)
            if n3:
                far_rhs[here] = chosen(
                    m3_refs, starts3, pos3_ref[k], lambda pair, at: jnp.where(at_end, pair[0][at], pair[1][at])
                )

        column = amplitude_rows(column_ref, row_ref, occ_ref, row, batch, share)
        target = jnp.bitwise_xor(column, occ_ref[batch])
        if few:
            own, e1, o1, two, three = m2_refs
            half = share // 2
            lane = lax.broadcasted_iota(jnp.int32, (half, 2 * NARROW), 1)

            @pl.loop(0, fold_ref.shape[2] // share)
            def _(n):
                used = n < count_ref[0]
                first = pl.multiple_of(n * share, share)
                for slot, wanted, ref in ((0, used & at_end, three), (1, used, two)):
                    block = ref[n, 0]
                    zero = jnp.zeros_like(block)
                    block = jnp.where(wanted, block, zero)
                    third_rhs[slot, pl.ds(first, half)] = jnp.where(lane < NARROW, block, zero)
                    third_rhs[slot, pl.ds(first + half, half)] = jnp.where(lane < NARROW, zero, block)
                pieces = []
                for piece in range(2):
                    close = groups * K_STEP + 2 * n + piece
                    block = own[n, 1 + piece] + e1[close] + two[n, 1 + piece]
                    block = block + jnp.where(at_end, three[n, 1 + piece], o1[close])
                    pieces.append(jnp.where(used, block, jnp.zeros_like(block)))
                short = jnp.concatenate(pieces, axis=1)
                short_rhs[pl.ds(first, share)] = jnp.concatenate([short, short], axis=0)

            narrow = jnp.dot(fold_ref[0], third_rhs[0], preferred_element_type=jnp.float32)
            narrow += jnp.dot(fold_ref[1], third_rhs[1], preferred_element_type=jnp.float32)
            narrow_sum[...] = narrow_ref[...] + narrow
            total_ref[...] = wide_ref[...] + jnp.dot(
                fold_ref[2], short_rhs[...], preferred_element_type=jnp.float32
            )
        else:
            narrow_sum[...] = narrow_ref[...]

            @pl.when(at_end)
            def _():
                half = share // 2
                lane = lax.broadcasted_iota(jnp.int32, (half, 2 * NARROW), 1)

                @pl.loop(0, groups * K_STEP)
                def _(k):
                    block = e3_ref[k]
                    zero = jnp.zeros_like(block)
                    first = pl.multiple_of(k * share, share)
                    third_rhs[0, pl.ds(first, half)] = jnp.where(lane < NARROW, block, zero)
                    third_rhs[0, pl.ds(first + half, half)] = jnp.where(lane < NARROW, zero, block)

                @pl.loop(0, groups)
                def _(group):
                    rhs = third_rhs[0, pl.ds(pl.multiple_of(group * width, width), width)]
                    narrow_sum[...] += jnp.dot(third_ref[group], rhs, preferred_element_type=jnp.float32)

            total_ref[...] = wide_ref[...] if n3 else jnp.zeros(total_ref.shape, jnp.float32)
        @pl.loop(0, groups)
        def _(group):
            here = pl.ds(pl.multiple_of(group * width, width), width)
            if not few:
                total_ref[...] += jnp.dot(fold_ref[group], short_rhs[here], preferred_element_type=jnp.float32)
            if n3:
                total_ref[...] += jnp.dot(far_ref[group], far_rhs[here], preferred_element_type=jnp.float32)

        both = narrow_sum[...]
        both = both + pltpu.roll(both, NARROW, 1)
        both = jnp.concatenate([both] * (FOLD // (2 * NARROW)), axis=1)
        total_ref[...] = jnp.where(target == largest_irrep(vir_ref), total_ref[...], both)
        write_quarters(total_ref, col, outs)

    return kernel


def last_product(third_lhs, far_lhs, fold, occ_irrep, vir_irrep, pos2, pos3, count, place, narrow_sum, wide_sum, few, m2, m3, e3, batch):
    groups, rows, width = far_lhs.shape
    share = rows // batch
    vmem = pl.BlockSpec(memory_space=pltpu.VMEM)
    smem = pl.BlockSpec(memory_space=pltpu.SMEM)
    arrays = [narrow_sum, wide_sum] + list(m2) + [v for group in m3 for v in group] + list(e3)
    quarter = (batch // 2, share, FOLD // 2)
    whole = groups * width
    unused = jnp.zeros((16, 128), jnp.bfloat16)
    return pl.pallas_call(
        make_last_kernel(few, len(m2), starts_of(m2), len(m3), starts_of([v[0] for v in m3])),
        in_specs=[smem] * 6 + [vmem] * (4 + len(arrays)),
        out_specs=[vmem] * 4,
        out_shape=[jax.ShapeDtypeStruct(quarter, jnp.float32)] * 4,
        scratch_shapes=[
            pltpu.VMEM((vir_irrep.shape[0], 8), jnp.int32),
            pltpu.VMEM((rows, FOLD), jnp.float32),
            pltpu.VMEM((rows, 2 * NARROW), jnp.float32),
            pltpu.VMEM((fold.shape[2] if few else whole, FOLD), jnp.bfloat16),
            pltpu.VMEM((whole if m3 else 16, FOLD), jnp.bfloat16),
            pltpu.VMEM((2, fold.shape[2]) + (2 * NARROW,) if few else (1, whole, 2 * NARROW), jnp.bfloat16),
        ],
        cost_estimate=cost(4 if m3 else 3),
        compiler_params=pltpu.CompilerParams(vmem_limit_bytes=32 * 1024 * 1024),
    )(occ_irrep, vir_irrep, pos2, pos3, count, place, fold, unused if few else third_lhs,
      far_lhs if m3 else unused, vir_irrep[None, :], *arrays)


def dense_product(amplitudes, whole, occ_irrep, occ_local, vir_local, vir_irrep):
    batch = amplitudes.shape[0]
    keep = (
        jnp.bitwise_xor(occ_irrep[:batch, None], occ_local[None, :])[:, :, None, None]
        == jnp.bitwise_xor(vir_local[:, None], vir_irrep[None, :])[None, None]
    )
    kept = jnp.where(keep, amplitudes, jnp.zeros_like(amplitudes))
    return lax.dot_general(
        kept, whole, (((1, 3), (0, 1)), ((), ())), preferred_element_type=jnp.float32
    )


def finish(cycle, occ_irrep, vir_irrep, occ_energy, vir_energy, a_start, a_size, b_start, b_size, batch):
    label_a = lax.dynamic_slice_in_dim(vir_irrep, a_start, a_size)
    label_b = lax.dynamic_slice_in_dim(vir_irrep, b_start, b_size)
    energy_a = lax.dynamic_slice_in_dim(vir_energy, a_start, a_size)
    energy_b = lax.dynamic_slice_in_dim(vir_energy, b_start, b_size)
    target = jnp.bitwise_xor(
        jnp.bitwise_xor(occ_irrep[:batch, None], occ_irrep[batch]), label_a[None, :]
    )
    keep = label_b[:, None, None] == target[None, :, :]
    denominator = (
        occ_energy[:batch][None, :, None]
        + occ_energy[batch]
        - energy_a[None, None, :]
        - energy_b[:, None, None]
    )
    swapped = jnp.transpose(cycle, (2, 0, 1))
    return jnp.where(keep, swapped, 0.0) / denominator


def on_square(amplitudes, integrals, occ_irrep, vir_irrep, screen):
    batch, occ_share, share, vir_total = amplitudes.shape
    row = lax.axis_index("row")
    col = lax.axis_index("col")
    place = jnp.stack([row, col]).astype(jnp.int32)
    few, m2a, m2b, m3a, m3b, pos2, pos3, posx, form, count = wide_blocks(
        integrals, occ_irrep, vir_irrep, screen, place, batch
    )
    outer = [(0, 1), (1, 0), (2, 3), (3, 2)]
    inner = [(1, 2), (2, 1)]
    inward = [(0, 1), (3, 2)]
    outward = [(1, 0), (2, 3)]
    ends = [(0, 3), (3, 0)]
    second = [(r, r ^ 2) for r in range(4)]

    def move(v, pairs):
        return lax.ppermute(v, "row", pairs)

    def sparse(use_few, choose):
        def run(few, m2a, m2b, m3a, m3b):
            shorts, wides = choose(m2a, m2b, m3a, m3b)
            near = [(own, move(own, outer), move(own, inner)) for own in wides]
            few = few[:use_few] if use_few else None
            narrow = narrow_blocks(integrals, occ_irrep, vir_irrep, screen, place, few, batch)
            if use_few:
                e1, o1 = move(narrow, outer), move(narrow, inner)
                lhs, third_lhs, far_lhs, fold = masked_amplitudes(
                    amplitudes, occ_irrep, vir_irrep, place, posx, use_few
                )
                near, e1, o1, few, _ = lax.optimization_barrier((near, e1, o1, few, fold))
                two, three = move(few, second), move(few, ends)
                blocks, e3 = (narrow, e1, o1), []
                sums = (few, e1, o1, two, three)
            else:
                h1 = [move(v, inward) for v in shorts]
                o1, e1 = move(narrow, inner), move(narrow, outward)
                lhs, third_lhs, far_lhs, fold = masked_amplitudes(
                    amplitudes, occ_irrep, vir_irrep, place, posx, 0
                )
                near, h1, o1, e1, _ = lax.optimization_barrier((near, h1, o1, e1, fold))
                h2 = [move(own + v, inner) for own, v in zip(shorts, h1)]
                e1 = e1 + move(narrow, inward)
                e2 = move(o1, outward)
                h2, e1, e2 = lax.optimization_barrier((h2, e1, e2))
                h3 = [move(own + v, outward) for own, v in zip(shorts, h2)]
                o2 = move(e1, inner)
                blocks, e3 = (narrow, e1, o1, e2, o2), [move(o2, outward)]
                sums = [a + b + c + d for a, b, c, d in zip(shorts, h1, h2, h3)]
            far = [(move(o, outward), move(e, inner)) for _, e, o in near]
            narrow_sum, wide_sum = first_product(
                lhs, third_lhs, far_lhs, pos3, place, blocks, bool(use_few), near
            )
            return list(last_product(
                third_lhs, far_lhs, fold, occ_irrep, vir_irrep, pos2, pos3, count, place, narrow_sum, wide_sum,
                bool(use_few), sums, far, e3, batch
            ))

        return run

    def dense(*_):
        occ_local = lax.dynamic_slice_in_dim(occ_irrep, col * occ_share, occ_share)
        vir_local = lax.dynamic_slice_in_dim(vir_irrep, row * share, share)
        screen_rows = lax.dynamic_slice_in_dim(screen, col * occ_share, occ_share, 0)
        fold = folded_integrals(
            integrals, occ_local, vir_local, vir_irrep, occ_irrep[batch], screen_rows
        )
        whole = jnp.zeros((occ_share, vir_total, FOLD), fold.dtype)
        for s in range(4):
            block = move(fold, [(r, r ^ s) for r in range(4)]) if s else fold
            whole = lax.dynamic_update_slice_in_dim(whole, block, jnp.bitwise_xor(row, s) * share, 1)
        total = dense_product(amplitudes, whole, occ_irrep, occ_local, vir_local, vir_irrep)
        quarter = (batch // 2, share, FOLD // 2)
        goals = [jnp.bitwise_xor(col, t) for t in range(4)]
        return [
            lax.dynamic_slice(total, (g // 2 * quarter[0], 0, g % 2 * quarter[2]), quarter) for g in goals
        ]

    branches = [
        sparse(0, lambda m2a, m2b, m3a, m3b: ([m2a], [])),
        sparse(0, lambda m2a, m2b, m3a, m3b: ([m2a, m2b], [])),
        sparse(0, lambda m2a, m2b, m3a, m3b: ([m2a], [m3a[:FEW_WIDE]])),
        sparse(FEW_CAPS[0], lambda m2a, m2b, m3a, m3b: ([], [m3a])),
        sparse(FEW_CAPS[1], lambda m2a, m2b, m3a, m3b: ([], [m3a])),
        sparse(0, lambda m2a, m2b, m3a, m3b: ([m2a, m2b], [m3a, m3b])),
        dense,
    ]
    quarters = lax.switch(form[0], branches, few, m2a, m2b, m3a, m3b)
    mine = quarters[0]
    for t in (1, 2, 3):
        mine = mine + lax.ppermute(quarters[t], "col", [(q, q ^ t) for q in range(4)])
    places = [(r, q) for r in range(4) for q in range(4)]
    same = lax.ppermute(mine, ("row", "col"), [(r * 4 + q, q * 4 + r) for r, q in places])
    other = lax.ppermute(mine, ("row", "col"), [(r * 4 + q, (q ^ 2) * 4 + r) for r, q in places])
    upper = row // 2 == 1
    low = jnp.where(upper, other, same)
    high = jnp.where(upper, same, other)
    return jnp.concatenate([low, high], axis=0)


def on_any(amplitudes, integrals, occ_irrep, vir_irrep, screen):
    batch, occ_share, share, vir_total = amplitudes.shape
    row = lax.axis_index("row")
    col = lax.axis_index("col")
    occ_local = lax.dynamic_slice_in_dim(occ_irrep, col * occ_share, occ_share)
    vir_local = lax.dynamic_slice_in_dim(vir_irrep, row * share, share)
    screen_rows = lax.dynamic_slice_in_dim(screen, col * occ_share, occ_share, 0)
    fold = folded_integrals(
        integrals, occ_local, vir_local, vir_irrep, occ_irrep[batch], screen_rows
    )
    whole = lax.all_gather(fold, "row", axis=1, tiled=True)
    cycle = dense_product(amplitudes, whole, occ_irrep, occ_local, vir_local, vir_irrep)
    cycle = lax.psum(cycle, "col")
    cycle = jnp.concatenate([cycle] * (vir_total // FOLD), axis=2)
    cycle = lax.all_to_all(cycle, "row", split_axis=2, concat_axis=1, tiled=True)
    a_size = vir_total // lax.axis_size("col")
    return lax.dynamic_slice_in_dim(cycle, col * a_size, a_size, 1)


def on_device(amplitudes, integrals, occ_irrep, vir_irrep, screen, occ_energy, vir_energy):
    batch, _, vir_share, vir_total = amplitudes.shape
    square = lax.axis_size("row") == 4 and lax.axis_size("col") == 4
    form = on_square if square else on_any
    cycle = form(amplitudes, integrals, occ_irrep, vir_irrep, screen)
    a_size = vir_total // lax.axis_size("col")
    return finish(
        cycle, occ_irrep, vir_irrep, occ_energy, vir_energy,
        lax.axis_index("col") * a_size, a_size, lax.axis_index("row") * vir_share, vir_share, batch,
    )


def solution(mesh):
    in_specs = (
        P("parts", "col", "row", None),
        P(("parts", "col"), "row", None),
        P("parts"),
        P("parts"),
        P("parts", None),
        P("parts"),
        P("parts"),
    )
    out_specs = P("row", "parts", "col")
    return jax.shard_map(
        on_device, mesh=mesh, in_specs=in_specs, out_specs=out_specs, check_vma=False
    )
```

profile of v0, /device:TPU:1, one launch (start us, length us, event | category | flops | bytes accessed | tf_op | source)
XLA Modules:
  0.0 115.2 jit_solution(16869961012250757317)
XLA Ops:
  0.0 0.1 pad_add_fusion.refs_3_
  0.1 5.6 %shard_map.73 = (bf16[10,3,64,128]{3,2,1,0:T(8,128)(2,1)S(1)}, bf16[22,64,256]{2,1,0:T(8,128)(2,1)S(1)}, bf16[3,64,256]{2,1,0:T(8,128)(2,1)S(1)}, bf16[22,128,25...) custom-call(s32[100]{0:T(128)} %refs_0_.1, ...), custom_call_target="tpu_custom_call" | custom-call | flops 5000000000 | bytes 15000000 | tf_op jit(solution)/shard_map/pallas_call | solution.py:196
  6.4 89.2 %conditional.1 = (f32[2,128,128]{2,1,0:T(8,128)S(1)}, f32[2,128,128]{2,1,0:T(8,128)S(1)}, f32[2,128,128]{2,1,0:T(8,128)S(1)}, f32[2,128,128]{1,0,2:T(2,128)S(1)}) conditional(s32[]{:T(128)} %bitcast.21, (s32[512]{0:T(512)S(1)}, s32[100]{0:T(128)S(1)}, s32[2]{0:T(128)S(1)}, s32[25]{0:T(128)S(1)}, ...), branch_computations={%region_0.0_spmd, %region_1.0_spmd, %region_2.0_spmd, %region_3.0_... | conditional | flops 24001843200 | bytes 157594528 | solution.py:708
  6.5 2.2 %collective-permute-start.37 = (bf16[7,128,256]{2,1,0:T(8,128)(2,1)S(1)}, bf16[7,128,256]{2,1,0:T(8,128)(2,1)S(1)}, u32[]{:S(2)}, u32[]{:S(2)}) collective-permute-start(bf16[7,128,256]{2,1,0:T(8,128)(2,1)S(1)} %slice.20.refs_5_), channel_id=1, source_target_pairs={{0,4},{4,0},{8,12},{12,8},{1,5},{5,1},{9,13},{13,9},{2,6},{6,2},{1... | collective-permute-start | bytes 1376264 | tf_op jit(solution)/shard_map/cond/branch_2_fun/ppermute | solution.py:638
  8.7 0.7 collective-permute-start.38
  9.4 5.8 %collective-permute-start.39 = (bf16[22,64,256]{2,1,0:T(8,128)(2,1)S(1)}, bf16[22,64,256]{2,1,0:T(8,128)(2,1)S(1)}, u32[]{:S(2)}, u32[]{:S(2)}) collective-permute-start(bf16[22,64,256]{2,1,0:T(8,128)(2,1)S(1)} %get-tuple-element.228), channel_id=1, source_target_pairs={{0,4},{12,8},{1,5},{13,9},{2,6},{14,10},{3,7},{15,11},{16,20},{28,... | collective-permute-start | bytes 2162696 | tf_op jit(solution)/shard_map/cond/branch_2_fun/ppermute | solution.py:638
  15.1 3.1 %branch_2_fun.5.refs_0_ = bf16[25,64,128]{2,1,0:T(8,128)(2,1)S(1)} custom-call(s32[100]{0:T(128)S(1)} %get-tuple-element.214.refs_0_.occ_ref, s32[512]{0:T(512)S(1)} %get-tuple-element.215.refs_1_.vir_ref, s32[8,100]{1,0:T(8,128)S(1)} %bitcast.76, s32[2]{0:T(128)S(1)} %get-tuple-element.219.refs_1_.refs_3_.place_ref, ...), custom_call_target="tpu_custom_call" | custom-call | flops 4000000000 | bytes 12000000 | tf_op jit(solution)/shard_map/cond/branch_2_fun/pallas_call | solution.py:250
  18.2 0.7 collective-permute-start.40
  18.9 1.3 %collective-permute-start.41 = (bf16[25,64,128]{2,1,0:T(8,128)(2,1)S(1)}, bf16[25,64,128]{2,1,0:T(8,128)(2,1)S(1)}, u32[]{:S(2)}, u32[]{:S(2)}) collective-permute-start(bf16[25,64,128]{2,1,0:T(8,128)(2,1)S(1)} %branch_2_fun.5.refs_0_), channel_id=1, source_target_pairs={{4,0},{8,12},{5,1},{9,13},{6,2},{10,14},{7,3},{11,15},{20,16},{24,... | collective-permute-start | bytes 1228808 | tf_op jit(solution)/shard_map/cond/branch_2_fun/ppermute | solution.py:638
  20.2 8.9 %branch_2_fun.4 = (bf16[5,512,1280]{2,1,0:T(8,128)(2,1)S(1)}, bf16[5,512,640]{2,1,0:T(8,128)(2,1)S(1)}, bf16[5,512,640]{2,1,0:T(8,128)(2,1)S(1)}, bf16[5,512,640]{2,1,0:T(8,128)(2,1)S(1)}) custom-call(s32[100]{0:T(128)S(1)} %get-tuple-element.214.refs_0_.occ_ref, s32[2]{0:T(128)S(1)} %get-tuple-element.219.refs_1_.refs_3_.place_ref, ...), custom_call_target="tpu_custom_call" | custom-call | flops 7000000000 | bytes 21000000 | tf_op jit(solution)/shard_map/cond/branch_2_fun/pallas_call | solution.py:377
  29.1 3.2 %collective-permute-done.41 = bf16[25,64,128]{2,1,0:T(8,128)(2,1)S(1)} collective-permute-done((bf16[25,64,128]{2,1,0:T(8,128)(2,1)S(1)}, bf16[25,64,128]{2,1,0:T(8,128)(2,1)S(1)}, u32[]{:S(2)}, u32[]{:S(2)}) %collective-permute-start.41) | collective-permute-done | bytes 409632 | tf_op jit(solution)/shard_map/cond/branch_2_fun/ppermute | solution.py:638
  32.4 1.9 %collective-permute-done.39 = bf16[22,64,256]{2,1,0:T(8,128)(2,1)S(1)} collective-permute-done((bf16[22,64,256]{2,1,0:T(8,128)(2,1)S(1)}, bf16[22,64,256]{2,1,0:T(8,128)(2,1)S(1)}, u32[]{:S(2)}, u32[]{:S(2)}) %collective-permute-start.39) | collective-permute-done | bytes 720928 | tf_op jit(solution)/shard_map/cond/branch_2_fun/ppermute | solution.py:638
  34.3 0.2 add.137
  34.5 0.7 collective-permute-start.42
  35.2 6.6 %collective-permute-start.43 = (bf16[25,64,128]{2,1,0:T(8,128)(2,1)S(1)}, bf16[25,64,128]{2,1,0:T(8,128)(2,1)S(1)}, u32[]{:S(2)}, u32[]{:S(2)}) collective-permute-start(bf16[25,64,128]{2,1,0:T(8,128)(2,1)S(1)} %branch_2_fun.5.refs_0_), channel_id=1, source_target_pairs={{0,4},{12,8},{1,5},{13,9},{2,6},{14,10},{3,7},{15,11},{16,20},{28,... | collective-permute-start | bytes 1228808 | tf_op jit(solution)/shard_map/cond/branch_2_fun/ppermute | solution.py:638
  41.9 1.5 %collective-permute-start.44 = (bf16[25,64,128]{2,1,0:T(8,128)(2,1)S(1)}, bf16[25,64,128]{2,1,0:T(8,128)(2,1)S(1)}, u32[]{:S(2)}, u32[]{:S(2)}) collective-permute-start(bf16[25,64,128]{2,1,0:T(8,128)(2,1)S(1)} %collective-permute-done.40.refs_2_), channel_id=1, source_target_pairs={{4,0},{8,12},{5,1},{9,13},{6,2},{10,14},{7,3},{11,15},{20,16},{24,... | collective-permute-start | bytes 1228808 | tf_op jit(solution)/shard_map/cond/branch_2_fun/ppermute | solution.py:638
  43.4 4.1 %collective-permute-done.43 = bf16[25,64,128]{2,1,0:T(8,128)(2,1)S(1)} collective-permute-done((bf16[25,64,128]{2,1,0:T(8,128)(2,1)S(1)}, bf16[25,64,128]{2,1,0:T(8,128)(2,1)S(1)}, u32[]{:S(2)}, u32[]{:S(2)}) %collective-permute-start.43) | collective-permute-done | bytes 409632 | tf_op jit(solution)/shard_map/cond/branch_2_fun/ppermute | solution.py:638
  47.5 0.1 add.138.refs_1_
  47.6 3.0 %collective-permute-done.44.refs_3_ = bf16[25,64,128]{2,1,0:T(8,128)(2,1)S(1)} collective-permute-done((bf16[25,64,128]{2,1,0:T(8,128)(2,1)S(1)}, bf16[25,64,128]{2,1,0:T(8,128)(2,1)S(1)}, u32[]{:S(2)}, u32[]{:S(2)}) %collective-permute-start.44) | collective-permute-done | bytes 409632 | tf_op jit(solution)/shard_map/cond/branch_2_fun/ppermute | solution.py:638
  50.6 0.7 collective-permute-start.45
  51.3 1.3 %collective-permute-start.47 = (bf16[7,128,256]{2,1,0:T(8,128)(2,1)S(1)}, bf16[7,128,256]{2,1,0:T(8,128)(2,1)S(1)}, u32[]{:S(2)}, u32[]{:S(2)}) collective-permute-start(bf16[7,128,256]{2,1,0:T(8,128)(2,1)S(1)} %collective-permute-done.38.refs_7_), channel_id=1, source_target_pairs={{4,0},{8,12},{5,1},{9,13},{6,2},{10,14},{7,3},{11,15},{20,16},{24,... | collective-permute-start | bytes 1376264 | tf_op jit(solution)/shard_map/cond/branch_2_fun/ppermute | solution.py:638
  52.6 0.7 collective-permute-start.48
  53.3 0.2 add.140
  53.5 1.3 %collective-permute-start.46 = (bf16[22,64,256]{2,1,0:T(8,128)(2,1)S(1)}, bf16[22,64,256]{2,1,0:T(8,128)(2,1)S(1)}, u32[]{:S(2)}, u32[]{:S(2)}) collective-permute-start(bf16[22,64,256]{2,1,0:T(8,128)(2,1)S(1)} %add.140), channel_id=1, source_target_pairs={{4,0},{8,12},{5,1},{9,13},{6,2},{10,14},{7,3},{11,15},{20,16},{24,... | collective-permute-start | bytes 2162696 | tf_op jit(solution)/shard_map/cond/branch_2_fun/ppermute | solution.py:638
  54.8 1.3 %collective-permute-start.49 = (bf16[25,64,128]{2,1,0:T(8,128)(2,1)S(1)}, bf16[25,64,128]{2,1,0:T(8,128)(2,1)S(1)}, u32[]{:S(2)}, u32[]{:S(2)}) collective-permute-start(bf16[25,64,128]{2,1,0:T(8,128)(2,1)S(1)} %collective-permute-done.45.refs_4_), channel_id=1, source_target_pairs={{4,0},{8,12},{5,1},{9,13},{6,2},{10,14},{7,3},{11,15},{20,16},{24,... | collective-permute-start | bytes 1228808 | tf_op jit(solution)/shard_map/cond/branch_2_fun/ppermute | solution.py:638
  56.1 9.0 %branch_2_fun.6 = (f32[512,128]{1,0:T(8,128)S(1)}, f32[512,256]{1,0:T(8,128)S(1)}) custom-call(s32[25]{0:T(128)S(1)} %get-tuple-element.217.pos3_ref, s32[2]{0:T(128)S(1)} %get-tuple-element.219.refs_1_.refs_3_.place_ref, bf16[5,512,1280]{2,1,0:T(8,128)(2,1)S(1)} %get-tuple-element.225.lhs_ref, bf16[5,512,640]{2,1,0:T(8,128)(2,1)S(1)} %get-tuple-element.223.third_ref, ...), custom_call_target="tpu_custom_call" | custom-call | flops 8999999488 | bytes 27000000 | tf_op jit(solution)/shard_map/cond/branch_2_fun/pallas_call | solution.py:451
  65.1 16.4 %collective-permute-done.46 = bf16[22,64,256]{2,1,0:T(8,128)(2,1)S(1)} collective-permute-done((bf16[22,64,256]{2,1,0:T(8,128)(2,1)S(1)}, bf16[22,64,256]{2,1,0:T(8,128)(2,1)S(1)}, u32[]{:S(2)}, u32[]{:S(2)}) %collective-permute-start.46) | collective-permute-done | bytes 720928 | tf_op jit(solution)/shard_map/cond/branch_2_fun/ppermute | solution.py:638
  81.5 0.1 add_add_fusion.3.refs_0_
  81.7 6.4 %collective-permute-done.49.refs_3_ = bf16[25,64,128]{2,1,0:T(8,128)(2,1)S(1)} collective-permute-done((bf16[25,64,128]{2,1,0:T(8,128)(2,1)S(1)}, bf16[25,64,128]{2,1,0:T(8,128)(2,1)S(1)}, u32[]{:S(2)}, u32[]{:S(2)}) %collective-permute-start.49) | collective-permute-done | bytes 409632 | tf_op jit(solution)/shard_map/cond/branch_2_fun/ppermute | solution.py:638
  88.0 6.9 %branch_2_fun.7 = (f32[2,128,128]{2,1,0:T(8,128)S(1)}, f32[2,128,128]{2,1,0:T(8,128)S(1)}, f32[2,128,128]{2,1,0:T(8,128)S(1)}, f32[2,128,128]{2,1,0:T(8,128)S(1)}) custom-call(s32[100]{0:T(128)S(1)} %get-tuple-element.214.refs_0_.occ_ref, s32[512]{0:T(512)S(1)} %get-tuple-element.215.refs_1_.vir_ref, s32[25]{0:T(128)S(1)} %get-tuple-element.216.pos2_ref, ...), custom_call_target="tpu_custom_call" | custom-call | flops 4000000000 | bytes 12000000 | tf_op jit(solution)/shard_map/cond/branch_2_fun/pallas_call | solution.py:572
  95.0 0.1 copy.21
  95.6 0.1 copy.17
  95.7 0.1 collective-permute-start.75
  95.8 0.1 copy.16
  96.0 0.1 copy.14
  96.1 2.2 %collective-permute-start.73 = (f32[2,128,128]{1,0,2:T(2,128)S(1)}, f32[2,128,128]{1,0,2:T(2,128)S(1)}, u32[]{:S(2)}, u32[]{:S(2)}) collective-permute-start(f32[2,128,128]{1,0,2:T(2,128)S(1)} %copy.14), channel_id=1, source_target_pairs={{0,1},{1,0},{2,3},{3,2},{4,5},{5,4},{6,7},{7,6},{8,9},{9,8},{10,11... | collective-permute-start | bytes 393224 | tf_op jit(solution)/shard_map/ppermute | solution.py:711
  98.3 0.6 slice.31
  99.0 0.6 slice.33
  99.5 0.6 slice_add_fusion.1
  100.2 0.1 fusion.13
  100.4 0.7 slice_xor_fusion
  101.1 0.1 fusion.12
  101.1 0.1 collective-permute-done.75
  101.3 4.5 %collective-permute-start.76 = (f32[2,128,128]{1,0,2:T(2,128)S(1)}, f32[2,128,128]{1,0,2:T(2,128)S(1)}, u32[]{:S(2)}, u32[]{:S(2)}) collective-permute-start(f32[2,128,128]{1,0,2:T(2,128)S(1)} %bitcast.50), channel_id=1, source_target_pairs={{0,8},{1,12},{2,0},{3,4},{4,9},{5,13},{6,1},{7,5},{8,10},{9,14},{1... | collective-permute-start | bytes 393224 | tf_op jit(solution)/shard_map/ppermute | solution.py:714
  105.8 1.9 %collective-permute-start.77 = (f32[2,128,128]{1,0,2:T(2,128)S(1)}, f32[2,128,128]{1,0,2:T(2,128)S(1)}, u32[]{:S(2)}, u32[]{:S(2)}) collective-permute-start(f32[2,128,128]{1,0,2:T(2,128)S(1)} %bitcast.51), channel_id=1, source_target_pairs={{0,0},{1,4},{2,8},{3,12},{4,1},{5,5},{6,9},{7,13},{8,2},{9,6},{10,... | collective-permute-start | bytes 393224 | tf_op jit(solution)/shard_map/ppermute | solution.py:713
  107.7 0.1 broadcast_xor_fusion.2
  107.8 6.3 %collective-permute-done.77 = f32[2,128,128]{1,0,2:T(2,128)S(1)} collective-permute-done((f32[2,128,128]{1,0,2:T(2,128)S(1)}, f32[2,128,128]{1,0,2:T(2,128)S(1)}, u32[]{:S(2)}, u32[]{:S(2)}) %collective-permute-start.77) | collective-permute-done | bytes 131104 | tf_op jit(solution)/shard_map/ppermute | solution.py:713
  114.2 1.0 fusion.11
  (25 shorter events, 0.3 us)
Async XLA Ops:
  0.1 6.3 %copy-start.3 = (s32[512]{0:T(512)S(1)}, s32[512]{0:T(512)}, u32[]{:S(2)}) copy-start(s32[512]{0:T(512)} %refs_1_.1) | copy-start | bytes 6148
  0.1 6.3 %copy-start.4 = (s32[100,8]{0,1:T(8,128)S(1)}, s32[100,8]{0,1:T(8,128)}, u32[]{:S(2)}) copy-start(s32[100,8]{0,1:T(8,128)} %param.18) | copy-start | bytes 9604
  0.1 6.3 %copy-start.5 = (s32[100]{0:T(128)S(1)}, s32[100]{0:T(128)}, u32[]{:S(2)}) copy-start(s32[100]{0:T(128)} %refs_0_.1) | copy-start | bytes 1204
  6.4 92.6 %copy-start.7 = (f32[100]{0:T(128)S(1)}, f32[100]{0:T(128)}, u32[]{:S(2)}) copy-start(f32[100]{0:T(128)} %param.19) | copy-start | bytes 1204
  6.4 93.8 %copy-start.6 = (f32[512]{0:T(512)S(1)}, f32[512]{0:T(512)}, u32[]{:S(2)}) copy-start(f32[512]{0:T(512)} %param.20) | copy-start | bytes 6148
  6.5 25.8 %collective-permute-start.37 = (bf16[7,128,256]{2,1,0:T(8,128)(2,1)S(1)}, bf16[7,128,256]{2,1,0:T(8,128)(2,1)S(1)}, u32[]{:S(2)}, u32[]{:S(2)}) collective-permute-start(bf16[7,128,256]{2,1,0:T(8,128)(2,1)S(1)} %slice.20.refs_5_), channel_id=1, source_target_pairs={{0,4},{4,0},{8,12},{12,8},{1,5},{5,1},{9,13},{13,9},{2,6},{6,2},{1... | collective-permute-start | bytes 1376264 | tf_op jit(solution)/shard_map/cond/branch_2_fun/ppermute | solution.py:638
  8.7 23.7 %collective-permute-start.38 = (bf16[7,128,256]{2,1,0:T(8,128)(2,1)S(1)}, bf16[7,128,256]{2,1,0:T(8,128)(2,1)S(1)}, u32[]{:S(2)}, u32[]{:S(2)}) collective-permute-start(bf16[7,128,256]{2,1,0:T(8,128)(2,1)S(1)} %slice.20.refs_5_), channel_id=1, source_target_pairs={{4,8},{8,4},{5,9},{9,5},{6,10},{10,6},{7,11},{11,7},{20,24},{24,20... | collective-permute-start | bytes 1376264 | tf_op jit(solution)/shard_map/cond/branch_2_fun/ppermute | solution.py:638
  9.4 24.9 %collective-permute-start.39 = (bf16[22,64,256]{2,1,0:T(8,128)(2,1)S(1)}, bf16[22,64,256]{2,1,0:T(8,128)(2,1)S(1)}, u32[]{:S(2)}, u32[]{:S(2)}) collective-permute-start(bf16[22,64,256]{2,1,0:T(8,128)(2,1)S(1)} %get-tuple-element.228), channel_id=1, source_target_pairs={{0,4},{12,8},{1,5},{13,9},{2,6},{14,10},{3,7},{15,11},{16,20},{28,... | collective-permute-start | bytes 2162696 | tf_op jit(solution)/shard_map/cond/branch_2_fun/ppermute | solution.py:638
  18.2 10.9 %collective-permute-start.40 = (bf16[25,64,128]{2,1,0:T(8,128)(2,1)S(1)}, bf16[25,64,128]{2,1,0:T(8,128)(2,1)S(1)}, u32[]{:S(2)}, u32[]{:S(2)}) collective-permute-start(bf16[25,64,128]{2,1,0:T(8,128)(2,1)S(1)} %branch_2_fun.5.refs_0_), channel_id=1, source_target_pairs={{4,8},{8,4},{5,9},{9,5},{6,10},{10,6},{7,11},{11,7},{20,24},{24,20... | collective-permute-start | bytes 1228808 | tf_op jit(solution)/shard_map/cond/branch_2_fun/ppermute | solution.py:638
  18.9 13.4 %collective-permute-start.41 = (bf16[25,64,128]{2,1,0:T(8,128)(2,1)S(1)}, bf16[25,64,128]{2,1,0:T(8,128)(2,1)S(1)}, u32[]{:S(2)}, u32[]{:S(2)}) collective-permute-start(bf16[25,64,128]{2,1,0:T(8,128)(2,1)S(1)} %branch_2_fun.5.refs_0_), channel_id=1, source_target_pairs={{4,0},{8,12},{5,1},{9,13},{6,2},{10,14},{7,3},{11,15},{20,16},{24,... | collective-permute-start | bytes 1228808 | tf_op jit(solution)/shard_map/cond/branch_2_fun/ppermute | solution.py:638
  34.5 16.1 %collective-permute-start.42 = (bf16[22,64,256]{2,1,0:T(8,128)(2,1)S(1)}, bf16[22,64,256]{2,1,0:T(8,128)(2,1)S(1)}, u32[]{:S(2)}, u32[]{:S(2)}) collective-permute-start(bf16[22,64,256]{2,1,0:T(8,128)(2,1)S(1)} %add.137), channel_id=1, source_target_pairs={{4,8},{8,4},{5,9},{9,5},{6,10},{10,6},{7,11},{11,7},{20,24},{24,20... | collective-permute-start | bytes 2162696 | tf_op jit(solution)/shard_map/cond/branch_2_fun/ppermute | solution.py:638
  35.2 12.2 %collective-permute-start.43 = (bf16[25,64,128]{2,1,0:T(8,128)(2,1)S(1)}, bf16[25,64,128]{2,1,0:T(8,128)(2,1)S(1)}, u32[]{:S(2)}, u32[]{:S(2)}) collective-permute-start(bf16[25,64,128]{2,1,0:T(8,128)(2,1)S(1)} %branch_2_fun.5.refs_0_), channel_id=1, source_target_pairs={{0,4},{12,8},{1,5},{13,9},{2,6},{14,10},{3,7},{15,11},{16,20},{28,... | collective-permute-start | bytes 1228808 | tf_op jit(solution)/shard_map/cond/branch_2_fun/ppermute | solution.py:638
  41.9 8.7 %collective-permute-start.44 = (bf16[25,64,128]{2,1,0:T(8,128)(2,1)S(1)}, bf16[25,64,128]{2,1,0:T(8,128)(2,1)S(1)}, u32[]{:S(2)}, u32[]{:S(2)}) collective-permute-start(bf16[25,64,128]{2,1,0:T(8,128)(2,1)S(1)} %collective-permute-done.40.refs_2_), channel_id=1, source_target_pairs={{4,0},{8,12},{5,1},{9,13},{6,2},{10,14},{7,3},{11,15},{20,16},{24,... | collective-permute-start | bytes 1228808 | tf_op jit(solution)/shard_map/cond/branch_2_fun/ppermute | solution.py:638
  50.6 4.2 %collective-permute-start.45 = (bf16[25,64,128]{2,1,0:T(8,128)(2,1)S(1)}, bf16[25,64,128]{2,1,0:T(8,128)(2,1)S(1)}, u32[]{:S(2)}, u32[]{:S(2)}) collective-permute-start(bf16[25,64,128]{2,1,0:T(8,128)(2,1)S(1)} %add.138.refs_1_), channel_id=1, source_target_pairs={{4,8},{8,4},{5,9},{9,5},{6,10},{10,6},{7,11},{11,7},{20,24},{24,20... | collective-permute-start | bytes 1228808 | tf_op jit(solution)/shard_map/cond/branch_2_fun/ppermute | solution.py:638
  51.3 30.4 %collective-permute-start.47 = (bf16[7,128,256]{2,1,0:T(8,128)(2,1)S(1)}, bf16[7,128,256]{2,1,0:T(8,128)(2,1)S(1)}, u32[]{:S(2)}, u32[]{:S(2)}) collective-permute-start(bf16[7,128,256]{2,1,0:T(8,128)(2,1)S(1)} %collective-permute-done.38.refs_7_), channel_id=1, source_target_pairs={{4,0},{8,12},{5,1},{9,13},{6,2},{10,14},{7,3},{11,15},{20,16},{24,... | collective-permute-start | bytes 1376264 | tf_op jit(solution)/shard_map/cond/branch_2_fun/ppermute | solution.py:638
  52.6 29.1 %collective-permute-start.48 = (bf16[7,128,256]{2,1,0:T(8,128)(2,1)S(1)}, bf16[7,128,256]{2,1,0:T(8,128)(2,1)S(1)}, u32[]{:S(2)}, u32[]{:S(2)}) collective-permute-start(bf16[7,128,256]{2,1,0:T(8,128)(2,1)S(1)} %collective-permute-done.37.refs_6_), channel_id=1, source_target_pairs={{4,8},{8,4},{5,9},{9,5},{6,10},{10,6},{7,11},{11,7},{20,24},{24,20... | collective-permute-start | bytes 1376264 | tf_op jit(solution)/shard_map/cond/branch_2_fun/ppermute | solution.py:638
  53.5 28.0 %collective-permute-start.46 = (bf16[22,64,256]{2,1,0:T(8,128)(2,1)S(1)}, bf16[22,64,256]{2,1,0:T(8,128)(2,1)S(1)}, u32[]{:S(2)}, u32[]{:S(2)}) collective-permute-start(bf16[22,64,256]{2,1,0:T(8,128)(2,1)S(1)} %add.140), channel_id=1, source_target_pairs={{4,0},{8,12},{5,1},{9,13},{6,2},{10,14},{7,3},{11,15},{20,16},{24,... | collective-permute-start | bytes 2162696 | tf_op jit(solution)/shard_map/cond/branch_2_fun/ppermute | solution.py:638
  54.8 33.2 %collective-permute-start.49 = (bf16[25,64,128]{2,1,0:T(8,128)(2,1)S(1)}, bf16[25,64,128]{2,1,0:T(8,128)(2,1)S(1)}, u32[]{:S(2)}, u32[]{:S(2)}) collective-permute-start(bf16[25,64,128]{2,1,0:T(8,128)(2,1)S(1)} %collective-permute-done.45.refs_4_), channel_id=1, source_target_pairs={{4,0},{8,12},{5,1},{9,13},{6,2},{10,14},{7,3},{11,15},{20,16},{24,... | collective-permute-start | bytes 1228808 | tf_op jit(solution)/shard_map/cond/branch_2_fun/ppermute | solution.py:638
  95.7 5.5 %collective-permute-start.75 = (f32[2,128,128]{1,0,2:T(2,128)S(1)}, f32[2,128,128]{1,0,2:T(2,128)S(1)}, u32[]{:S(2)}, u32[]{:S(2)}) collective-permute-start(f32[2,128,128]{1,0,2:T(2,128)S(1)} %copy.17), channel_id=1, source_target_pairs={{0,3},{1,2},{2,1},{3,0},{4,7},{5,6},{6,5},{7,4},{8,11},{9,10},{10,... | collective-permute-start | bytes 393224 | tf_op jit(solution)/shard_map/ppermute | solution.py:711
  95.9 5.3 %collective-permute-start.74 = (f32[2,128,128]{1,0,2:T(2,128)S(1)}, f32[2,128,128]{1,0,2:T(2,128)S(1)}, u32[]{:S(2)}, u32[]{:S(2)}) collective-permute-start(f32[2,128,128]{1,0,2:T(2,128)S(1)} %copy.16), channel_id=1, source_target_pairs={{0,2},{1,3},{2,0},{3,1},{4,6},{5,7},{6,4},{7,5},{8,10},{9,11},{10,... | collective-permute-start | bytes 393224 | tf_op jit(solution)/shard_map/ppermute | solution.py:711
  96.1 5.1 %collective-permute-start.73 = (f32[2,128,128]{1,0,2:T(2,128)S(1)}, f32[2,128,128]{1,0,2:T(2,128)S(1)}, u32[]{:S(2)}, u32[]{:S(2)}) collective-permute-start(f32[2,128,128]{1,0,2:T(2,128)S(1)} %copy.14), channel_id=1, source_target_pairs={{0,1},{1,0},{2,3},{3,2},{4,5},{5,4},{6,7},{7,6},{8,9},{9,8},{10,11... | collective-permute-start | bytes 393224 | tf_op jit(solution)/shard_map/ppermute | solution.py:711
  101.3 6.5 %collective-permute-start.76 = (f32[2,128,128]{1,0,2:T(2,128)S(1)}, f32[2,128,128]{1,0,2:T(2,128)S(1)}, u32[]{:S(2)}, u32[]{:S(2)}) collective-permute-start(f32[2,128,128]{1,0,2:T(2,128)S(1)} %bitcast.50), channel_id=1, source_target_pairs={{0,8},{1,12},{2,0},{3,4},{4,9},{5,13},{6,1},{7,5},{8,10},{9,14},{1... | collective-permute-start | bytes 393224 | tf_op jit(solution)/shard_map/ppermute | solution.py:714
  105.8 8.3 %collective-permute-start.77 = (f32[2,128,128]{1,0,2:T(2,128)S(1)}, f32[2,128,128]{1,0,2:T(2,128)S(1)}, u32[]{:S(2)}, u32[]{:S(2)}) collective-permute-start(f32[2,128,128]{1,0,2:T(2,128)S(1)} %bitcast.51), channel_id=1, source_target_pairs={{0,0},{1,4},{2,8},{3,12},{4,1},{5,5},{6,9},{7,13},{8,2},{9,6},{10,... | collective-permute-start | bytes 393224 | tf_op jit(solution)/shard_map/ppermute | solution.py:713
where the time goes:
time: 116 us; the launch traced here: 115 us
  waiting for transfers between devices  41.4 us (36%)
  Pallas kernels  33.5 us (29%)
  starting transfers between devices  33.4 us (29%)
  other arithmetic  3.37 us (3%)
  local copies, waits for them, and re-layouts  1.9 us (2%)
    ppermute x13, waiting for transfers between devices, move(): return lax.ppermute(v, 'row', pairs)  35 us
    ppermute x13, starting transfers between devices, move(): return lax.ppermute(v, 'row', pairs)  24.7 us
    pallas_call x1, Pallas kernels, first_product(): pl.pallas_call(make_first_kernel(few, len(m3), starts_of([v[0] for v in m...  9.02 us
    pallas_call x1, Pallas kernels, masked_amplitudes(): pl.pallas_call(kernel, in_specs=[smem, smem, smem, hbm, vmem], out_specs=...  8.91 us
    pallas_call x1, Pallas kernels, last_product(): pl.pallas_call(make_last_kernel(few, len(m2), starts_of(m2), len(m3), sta...  6.93 us
    ppermute x1, waiting for transfers between devices, on_square(): lax.ppermute(mine, ('row', 'col'), [(r * 4 + q, q * 4 + r) for r, q in pl...  6.34 us
    pallas_call x1, Pallas kernels, wide_blocks(): pl.pallas_call(kernel, in_specs=[smem] * 4 + [pl.BlockSpec(memory_space=p...  5.6 us
    ppermute x1, starting transfers between devices, on_square(): lax.ppermute(mine, ('row', 'col'), [(r * 4 + q, (q ^ 2) * 4 + r) for r, q...  4.54 us
  transfers between devices with their start and end apart: 18, of which 8 were waited for; matrix products, arithmetic and copies ran while one was open for 3% of the time, Pallas kernels for 18%

commit v1 on v0

--- a/solution.py
+++ b/solution.py
@@ -648,7 +648,7 @@
                 lhs, third_lhs, far_lhs, fold = masked_amplitudes(
                     amplitudes, occ_irrep, vir_irrep, place, posx, use_few
                 )
-                near, e1, o1, few, _ = lax.optimization_barrier((near, e1, o1, few, fold))
+                near, few, _ = lax.optimization_barrier((near, few, fold))
                 two, three = move(few, second), move(few, ends)
                 blocks, e3 = (narrow, e1, o1), []
                 sums = (few, e1, o1, two, three)

time: 116 us -> 114 us (0.983)
  the two profiles are of different devices: /device:TPU:1 before, /device:TPU:2 now
where the time goes in v1:
time: 114 us; the launch traced here: 112 us
  waiting for transfers between devices  44.7 us (39%)
  starting transfers between devices  32.9 us (29%)
  Pallas kernels  28 us (25%)
  other arithmetic  3.36 us (3%)
  local copies, waits for them, and re-layouts  1.87 us (2%)
    ppermute x9, waiting for transfers between devices, move(): return lax.ppermute(v, 'row', pairs)  33.1 us
    ppermute x9, starting transfers between devices, move(): return lax.ppermute(v, 'row', pairs)  16.7 us
    ppermute x3, starting transfers between devices, on_square(): lax.ppermute(quarters[t], 'col', [(q, q ^ t) for q in range(4)])  13.4 us
    pallas_call x1, Pallas kernels, masked_amplitudes(): pl.pallas_call(kernel, in_specs=[smem, smem, smem, hbm, vmem], out_specs=...  8.91 us
    pallas_call x1, Pallas kernels, last_product(): pl.pallas_call(make_last_kernel(few, len(m2), starts_of(m2), len(m3), sta...  5.76 us
    pallas_call x1, Pallas kernels, first_product(): pl.pallas_call(make_first_kernel(few, len(m3), starts_of([v[0] for v in m...  5.6 us
    ppermute x1, waiting for transfers between devices, on_square(): lax.ppermute(mine, ('row', 'col'), [(r * 4 + q, (q ^ 2) * 4 + r) for r, q...  4.81 us
    pallas_call x1, Pallas kernels, wide_blocks(): pl.pallas_call(kernel, in_specs=[smem] * 4 + [pl.BlockSpec(memory_space=p...  4.63 us
  transfers between devices with their start and end apart: 14, of which 8 were waited for; matrix products, arithmetic and copies ran while one was open for 3% of the time, Pallas kernels for 16%

profile of v1, /device:TPU:2, one launch (start us, length us, event | category | flops | bytes accessed | tf_op | source)
XLA Modules:
  0.0 112.3 jit_solution(7232317148039703125)
XLA Ops:
  0.0 0.1 pad_add_fusion.refs_3_
  0.1 4.6 %shard_map.73 = (bf16[10,3,64,128]{3,2,1,0:T(8,128)(2,1)S(1)}, bf16[22,64,256]{2,1,0:T(8,128)(2,1)S(1)}, bf16[3,64,256]{2,1,0:T(8,128)(2,1)S(1)}, bf16[22,128,25...) custom-call(s32[100]{0:T(128)} %refs_0_.1, ...), custom_call_target="tpu_custom_call" | custom-call | flops 5000000000 | bytes 15000000 | tf_op jit(solution)/shard_map/pallas_call | solution.py:196
  5.4 0.0 copy-start.7
  5.4 0.0 copy-start.6
  5.5 74.6 %conditional.1 = (f32[2,128,128]{2,1,0:T(8,128)S(1)}, f32[2,128,128]{2,1,0:T(8,128)S(1)}, f32[2,128,128]{2,1,0:T(8,128)S(1)}, f32[2,128,128]{1,0,2:T(2,128)S(1)}) conditional(s32[]{:T(128)} %bitcast.21, (s32[512]{0:T(512)S(1)}, s32[100]{0:T(128)S(1)}, s32[2]{0:T(128)S(1)}, s32[25]{0:T(128)S(1)}, ...), branch_computations={%region_0.0_spmd, %region_1.0_spmd, %region_2.0_spmd, %region_3.0_... | conditional | flops 24001843200 | bytes 157594528 | solution.py:708
  5.5 3.5 %collective-permute-start.16 = (bf16[22,64,256]{2,1,0:T(8,128)(2,1)S(1)}, bf16[22,64,256]{2,1,0:T(8,128)(2,1)S(1)}, u32[]{:S(2)}, u32[]{:S(2)}) collective-permute-start(bf16[22,64,256]{2,1,0:T(8,128)(2,1)S(1)} %get-tuple-element.179), channel_id=1, source_target_pairs={{0,4},{12,8},{1,5},{13,9},{2,6},{14,10},{3,7},{15,11},{16,20},{28,... | collective-permute-start | bytes 2162696 | tf_op jit(solution)/shard_map/cond/branch_0_fun/ppermute | solution.py:638
  9.0 3.1 %branch_0_fun.5.refs_0_ = bf16[25,64,128]{2,1,0:T(8,128)(2,1)S(1)} custom-call(s32[100]{0:T(128)S(1)} %get-tuple-element.165.refs_0_.occ_ref, s32[512]{0:T(512)S(1)} %get-tuple-element.166.refs_1_.vir_ref, s32[8,100]{1,0:T(8,128)S(1)} %bitcast.74, s32[2]{0:T(128)S(1)} %get-tuple-element.170.refs_1_.refs_3_.place_ref, ...), custom_call_target="tpu_custom_call" | custom-call | flops 4000000000 | bytes 12000000 | tf_op jit(solution)/shard_map/cond/branch_0_fun/pallas_call | solution.py:250
  12.1 0.7 collective-permute-start.17
  12.8 1.3 %collective-permute-start.18 = (bf16[25,64,128]{2,1,0:T(8,128)(2,1)S(1)}, bf16[25,64,128]{2,1,0:T(8,128)(2,1)S(1)}, u32[]{:S(2)}, u32[]{:S(2)}) collective-permute-start(bf16[25,64,128]{2,1,0:T(8,128)(2,1)S(1)} %branch_0_fun.5.refs_0_), channel_id=1, source_target_pairs={{4,0},{8,12},{5,1},{9,13},{6,2},{10,14},{7,3},{11,15},{20,16},{24,... | collective-permute-start | bytes 1228808 | tf_op jit(solution)/shard_map/cond/branch_0_fun/ppermute | solution.py:638
  14.1 8.9 %branch_0_fun.4 = (bf16[5,512,1280]{2,1,0:T(8,128)(2,1)S(1)}, bf16[5,512,640]{2,1,0:T(8,128)(2,1)S(1)}, bf16[5,512,640]{2,1,0:T(8,128)(2,1)S(1)}, bf16[5,512,640]{2,1,0:T(8,128)(2,1)S(1)}) custom-call(s32[100]{0:T(128)S(1)} %get-tuple-element.165.refs_0_.occ_ref, s32[2]{0:T(128)S(1)} %get-tuple-element.170.refs_1_.refs_3_.place_ref, ...), custom_call_target="tpu_custom_call" | custom-call | flops 7000000000 | bytes 21000000 | tf_op jit(solution)/shard_map/cond/branch_0_fun/pallas_call | solution.py:377
  23.0 2.5 %collective-permute-done.18 = bf16[25,64,128]{2,1,0:T(8,128)(2,1)S(1)} collective-permute-done((bf16[25,64,128]{2,1,0:T(8,128)(2,1)S(1)}, bf16[25,64,128]{2,1,0:T(8,128)(2,1)S(1)}, u32[]{:S(2)}, u32[]{:S(2)}) %collective-permute-start.18) | collective-permute-done | bytes 409632 | tf_op jit(solution)/shard_map/cond/branch_0_fun/ppermute | solution.py:638
  25.5 0.2 add.123
  25.8 0.7 collective-permute-start.19
  26.5 5.9 %collective-permute-start.20 = (bf16[25,64,128]{2,1,0:T(8,128)(2,1)S(1)}, bf16[25,64,128]{2,1,0:T(8,128)(2,1)S(1)}, u32[]{:S(2)}, u32[]{:S(2)}) collective-permute-start(bf16[25,64,128]{2,1,0:T(8,128)(2,1)S(1)} %branch_0_fun.5.refs_0_), channel_id=1, source_target_pairs={{0,4},{12,8},{1,5},{13,9},{2,6},{14,10},{3,7},{15,11},{16,20},{28,... | collective-permute-start | bytes 1228808 | tf_op jit(solution)/shard_map/cond/branch_0_fun/ppermute | solution.py:638
  32.4 1.3 %collective-permute-start.21 = (bf16[25,64,128]{2,1,0:T(8,128)(2,1)S(1)}, bf16[25,64,128]{2,1,0:T(8,128)(2,1)S(1)}, u32[]{:S(2)}, u32[]{:S(2)}) collective-permute-start(bf16[25,64,128]{2,1,0:T(8,128)(2,1)S(1)} %collective-permute-done.17.refs_2_), channel_id=1, source_target_pairs={{4,0},{8,12},{5,1},{9,13},{6,2},{10,14},{7,3},{11,15},{20,16},{24,... | collective-permute-start | bytes 1228808 | tf_op jit(solution)/shard_map/cond/branch_0_fun/ppermute | solution.py:638
  33.7 6.2 %collective-permute-done.20 = bf16[25,64,128]{2,1,0:T(8,128)(2,1)S(1)} collective-permute-done((bf16[25,64,128]{2,1,0:T(8,128)(2,1)S(1)}, bf16[25,64,128]{2,1,0:T(8,128)(2,1)S(1)}, u32[]{:S(2)}, u32[]{:S(2)}) %collective-permute-start.20) | collective-permute-done | bytes 409632 | tf_op jit(solution)/shard_map/cond/branch_0_fun/ppermute | solution.py:638
  39.9 0.1 add.124.refs_1_
  40.1 4.0 %collective-permute-done.21.refs_3_ = bf16[25,64,128]{2,1,0:T(8,128)(2,1)S(1)} collective-permute-done((bf16[25,64,128]{2,1,0:T(8,128)(2,1)S(1)}, bf16[25,64,128]{2,1,0:T(8,128)(2,1)S(1)}, u32[]{:S(2)}, u32[]{:S(2)}) %collective-permute-start.21) | collective-permute-done | bytes 409632 | tf_op jit(solution)/shard_map/cond/branch_0_fun/ppermute | solution.py:638
  44.1 0.7 collective-permute-start.22
  44.8 0.2 add.126
  45.0 1.3 %collective-permute-start.23 = (bf16[22,64,256]{2,1,0:T(8,128)(2,1)S(1)}, bf16[22,64,256]{2,1,0:T(8,128)(2,1)S(1)}, u32[]{:S(2)}, u32[]{:S(2)}) collective-permute-start(bf16[22,64,256]{2,1,0:T(8,128)(2,1)S(1)} %add.126), channel_id=1, source_target_pairs={{4,0},{8,12},{5,1},{9,13},{6,2},{10,14},{7,3},{11,15},{20,16},{24,... | collective-permute-start | bytes 2162696 | tf_op jit(solution)/shard_map/cond/branch_0_fun/ppermute | solution.py:638
  46.3 1.3 %collective-permute-start.24 = (bf16[25,64,128]{2,1,0:T(8,128)(2,1)S(1)}, bf16[25,64,128]{2,1,0:T(8,128)(2,1)S(1)}, u32[]{:S(2)}, u32[]{:S(2)}) collective-permute-start(bf16[25,64,128]{2,1,0:T(8,128)(2,1)S(1)} %collective-permute-done.22.refs_4_), channel_id=1, source_target_pairs={{4,0},{8,12},{5,1},{9,13},{6,2},{10,14},{7,3},{11,15},{20,16},{24,... | collective-permute-start | bytes 1228808 | tf_op jit(solution)/shard_map/cond/branch_0_fun/ppermute | solution.py:638
  47.6 5.6 %branch_0_fun.6 = (f32[512,128]{1,0:T(8,128)S(1)}, f32[16,256]{1,0:T(8,128)S(1)}) custom-call(s32[25]{0:T(128)S(1)} %get-tuple-element.168.pos3_ref, s32[2]{0:T(128)S(1)} %get-tuple-element.170.refs_1_.refs_3_.place_ref, bf16[5,512,1280]{2,1,0:T(8,128)(2,1)S(1)} %get-tuple-element.175.lhs_ref, bf16[5,512,640]{2,1,0:T(8,128)(2,1)S(1)} %get-tuple-element.174.third_ref, ...), custom_call_target="tpu_custom_call" | custom-call | flops 6000000000 | bytes 18000000 | tf_op jit(solution)/shard_map/cond/branch_0_fun/pallas_call | solution.py:451
  53.2 14.7 %collective-permute-done.23 = bf16[22,64,256]{2,1,0:T(8,128)(2,1)S(1)} collective-permute-done((bf16[22,64,256]{2,1,0:T(8,128)(2,1)S(1)}, bf16[22,64,256]{2,1,0:T(8,128)(2,1)S(1)}, u32[]{:S(2)}, u32[]{:S(2)}) %collective-permute-start.23) | collective-permute-done | bytes 720928 | tf_op jit(solution)/shard_map/cond/branch_0_fun/ppermute | solution.py:638
  67.9 0.1 add_add_fusion.refs_0_
  68.0 5.6 %collective-permute-done.24.refs_1_ = bf16[25,64,128]{2,1,0:T(8,128)(2,1)S(1)} collective-permute-done((bf16[25,64,128]{2,1,0:T(8,128)(2,1)S(1)}, bf16[25,64,128]{2,1,0:T(8,128)(2,1)S(1)}, u32[]{:S(2)}, u32[]{:S(2)}) %collective-permute-start.24) | collective-permute-done | bytes 409632 | tf_op jit(solution)/shard_map/cond/branch_0_fun/ppermute | solution.py:638
  73.7 5.8 %branch_0_fun.7 = (f32[2,128,128]{2,1,0:T(8,128)S(1)}, f32[2,128,128]{2,1,0:T(8,128)S(1)}, f32[2,128,128]{2,1,0:T(8,128)S(1)}, f32[2,128,128]{2,1,0:T(8,128)S(1)}) custom-call(s32[100]{0:T(128)S(1)} %get-tuple-element.165.refs_0_.occ_ref, s32[512]{0:T(512)S(1)} %get-tuple-element.166.refs_1_.vir_ref, s32[25]{0:T(128)S(1)} %get-tuple-element.167.pos2_ref, ...), custom_call_target="tpu_custom_call" | custom-call | flops 3000000000 | bytes 9000000 | tf_op jit(solution)/shard_map/cond/branch_0_fun/pallas_call | solution.py:572
  79.4 0.1 copy.19
  80.1 0.1 copy.17
  80.2 1.2 %collective-permute-start.75 = (f32[2,128,128]{1,0,2:T(2,128)S(1)}, f32[2,128,128]{1,0,2:T(2,128)S(1)}, u32[]{:S(2)}, u32[]{:S(2)}) collective-permute-start(f32[2,128,128]{1,0,2:T(2,128)S(1)} %copy.17), channel_id=1, source_target_pairs={{0,3},{1,2},{2,1},{3,0},{4,7},{5,6},{6,5},{7,4},{8,11},{9,10},{10,... | collective-permute-start | bytes 393224 | tf_op jit(solution)/shard_map/ppermute | solution.py:711
  81.4 0.1 copy.16
  81.6 12.0 %collective-permute-start.74 = (f32[2,128,128]{1,0,2:T(2,128)S(1)}, f32[2,128,128]{1,0,2:T(2,128)S(1)}, u32[]{:S(2)}, u32[]{:S(2)}) collective-permute-start(f32[2,128,128]{1,0,2:T(2,128)S(1)} %copy.16), channel_id=1, source_target_pairs={{0,2},{1,3},{2,0},{3,1},{4,6},{5,7},{6,4},{7,5},{8,10},{9,11},{10,... | collective-permute-start | bytes 393224 | tf_op jit(solution)/shard_map/ppermute | solution.py:711
  93.6 0.1 copy.14
  93.7 0.2 collective-permute-start.73
  93.8 0.6 slice.31
  94.5 0.6 slice.33
  95.1 0.6 slice_add_fusion.1
  95.7 0.1 fusion.13
  95.8 0.1 broadcast_subtract_fusion
  95.9 0.7 slice_xor_fusion
  96.6 0.1 fusion.12
  96.7 2.4 %collective-permute-done.74 = f32[2,128,128]{1,0,2:T(2,128)S(1)} collective-permute-done((f32[2,128,128]{1,0,2:T(2,128)S(1)}, f32[2,128,128]{1,0,2:T(2,128)S(1)}, u32[]{:S(2)}, u32[]{:S(2)}) %collective-permute-start.74) | collective-permute-done | bytes 131104 | tf_op jit(solution)/shard_map/ppermute | solution.py:711
  99.1 0.8 collective-permute-start.76
  100.0 1.9 %collective-permute-start.77 = (f32[2,128,128]{1,0,2:T(2,128)S(1)}, f32[2,128,128]{1,0,2:T(2,128)S(1)}, u32[]{:S(2)}, u32[]{:S(2)}) collective-permute-start(f32[2,128,128]{1,0,2:T(2,128)S(1)} %bitcast.51), channel_id=1, source_target_pairs={{0,0},{1,4},{2,8},{3,12},{4,1},{5,5},{6,9},{7,13},{8,2},{9,6},{10,... | collective-permute-start | bytes 393224 | tf_op jit(solution)/shard_map/ppermute | solution.py:713
  101.9 0.1 broadcast_xor_fusion.2
  102.0 4.8 %collective-permute-done.76 = f32[2,128,128]{1,0,2:T(2,128)S(1)} collective-permute-done((f32[2,128,128]{1,0,2:T(2,128)S(1)}, f32[2,128,128]{1,0,2:T(2,128)S(1)}, u32[]{:S(2)}, u32[]{:S(2)}) %collective-permute-start.76) | collective-permute-done | bytes 131104 | tf_op jit(solution)/shard_map/ppermute | solution.py:714
  106.8 4.4 %collective-permute-done.77 = f32[2,128,128]{1,0,2:T(2,128)S(1)} collective-permute-done((f32[2,128,128]{1,0,2:T(2,128)S(1)}, f32[2,128,128]{1,0,2:T(2,128)S(1)}, u32[]{:S(2)}, u32[]{:S(2)}) %collective-permute-start.77) | collective-permute-done | bytes 131104 | tf_op jit(solution)/shard_map/ppermute | solution.py:713
  111.2 1.0 fusion.11
  (17 shorter events, 0.1 us)
Async XLA Ops:
  0.1 5.3 %copy-start.3 = (s32[512]{0:T(512)S(1)}, s32[512]{0:T(512)}, u32[]{:S(2)}) copy-start(s32[512]{0:T(512)} %refs_1_.1) | copy-start | bytes 6148
  0.1 5.3 %copy-start.4 = (s32[100,8]{0,1:T(8,128)S(1)}, s32[100,8]{0,1:T(8,128)}, u32[]{:S(2)}) copy-start(s32[100,8]{0,1:T(8,128)} %param.18) | copy-start | bytes 9604
  0.1 5.3 %copy-start.5 = (s32[100]{0:T(128)S(1)}, s32[100]{0:T(128)}, u32[]{:S(2)}) copy-start(s32[100]{0:T(128)} %refs_0_.1) | copy-start | bytes 1204
  5.4 89.1 %copy-start.7 = (f32[100]{0:T(128)S(1)}, f32[100]{0:T(128)}, u32[]{:S(2)}) copy-start(f32[100]{0:T(128)} %param.19) | copy-start | bytes 1204
  5.4 90.3 %copy-start.6 = (f32[512]{0:T(512)S(1)}, f32[512]{0:T(512)}, u32[]{:S(2)}) copy-start(f32[512]{0:T(512)} %param.20) | copy-start | bytes 6148
  5.5 20.1 %collective-permute-start.16 = (bf16[22,64,256]{2,1,0:T(8,128)(2,1)S(1)}, bf16[22,64,256]{2,1,0:T(8,128)(2,1)S(1)}, u32[]{:S(2)}, u32[]{:S(2)}) collective-permute-start(bf16[22,64,256]{2,1,0:T(8,128)(2,1)S(1)} %get-tuple-element.179), channel_id=1, source_target_pairs={{0,4},{12,8},{1,5},{13,9},{2,6},{14,10},{3,7},{15,11},{16,20},{28,... | collective-permute-start | bytes 2162696 | tf_op jit(solution)/shard_map/cond/branch_0_fun/ppermute | solution.py:638
  12.1 10.9 %collective-permute-start.17 = (bf16[25,64,128]{2,1,0:T(8,128)(2,1)S(1)}, bf16[25,64,128]{2,1,0:T(8,128)(2,1)S(1)}, u32[]{:S(2)}, u32[]{:S(2)}) collective-permute-start(bf16[25,64,128]{2,1,0:T(8,128)(2,1)S(1)} %branch_0_fun.5.refs_0_), channel_id=1, source_target_pairs={{4,8},{8,4},{5,9},{9,5},{6,10},{10,6},{7,11},{11,7},{20,24},{24,20... | collective-permute-start | bytes 1228808 | tf_op jit(solution)/shard_map/cond/branch_0_fun/ppermute | solution.py:638
  12.8 12.8 %collective-permute-start.18 = (bf16[25,64,128]{2,1,0:T(8,128)(2,1)S(1)}, bf16[25,64,128]{2,1,0:T(8,128)(2,1)S(1)}, u32[]{:S(2)}, u32[]{:S(2)}) collective-permute-start(bf16[25,64,128]{2,1,0:T(8,128)(2,1)S(1)} %branch_0_fun.5.refs_0_), channel_id=1, source_target_pairs={{4,0},{8,12},{5,1},{9,13},{6,2},{10,14},{7,3},{11,15},{20,16},{24,... | collective-permute-start | bytes 1228808 | tf_op jit(solution)/shard_map/cond/branch_0_fun/ppermute | solution.py:638
  25.8 18.3 %collective-permute-start.19 = (bf16[22,64,256]{2,1,0:T(8,128)(2,1)S(1)}, bf16[22,64,256]{2,1,0:T(8,128)(2,1)S(1)}, u32[]{:S(2)}, u32[]{:S(2)}) collective-permute-start(bf16[22,64,256]{2,1,0:T(8,128)(2,1)S(1)} %add.123), channel_id=1, source_target_pairs={{4,8},{8,4},{5,9},{9,5},{6,10},{10,6},{7,11},{11,7},{20,24},{24,20... | collective-permute-start | bytes 2162696 | tf_op jit(solution)/shard_map/cond/branch_0_fun/ppermute | solution.py:638
  26.5 13.4 %collective-permute-start.20 = (bf16[25,64,128]{2,1,0:T(8,128)(2,1)S(1)}, bf16[25,64,128]{2,1,0:T(8,128)(2,1)S(1)}, u32[]{:S(2)}, u32[]{:S(2)}) collective-permute-start(bf16[25,64,128]{2,1,0:T(8,128)(2,1)S(1)} %branch_0_fun.5.refs_0_), channel_id=1, source_target_pairs={{0,4},{12,8},{1,5},{13,9},{2,6},{14,10},{3,7},{15,11},{16,20},{28,... | collective-permute-start | bytes 1228808 | tf_op jit(solution)/shard_map/cond/branch_0_fun/ppermute | solution.py:638
  32.4 11.6 %collective-permute-start.21 = (bf16[25,64,128]{2,1,0:T(8,128)(2,1)S(1)}, bf16[25,64,128]{2,1,0:T(8,128)(2,1)S(1)}, u32[]{:S(2)}, u32[]{:S(2)}) collective-permute-start(bf16[25,64,128]{2,1,0:T(8,128)(2,1)S(1)} %collective-permute-done.17.refs_2_), channel_id=1, source_target_pairs={{4,0},{8,12},{5,1},{9,13},{6,2},{10,14},{7,3},{11,15},{20,16},{24,... | collective-permute-start | bytes 1228808 | tf_op jit(solution)/shard_map/cond/branch_0_fun/ppermute | solution.py:638
  44.1 2.2 %collective-permute-start.22 = (bf16[25,64,128]{2,1,0:T(8,128)(2,1)S(1)}, bf16[25,64,128]{2,1,0:T(8,128)(2,1)S(1)}, u32[]{:S(2)}, u32[]{:S(2)}) collective-permute-start(bf16[25,64,128]{2,1,0:T(8,128)(2,1)S(1)} %add.124.refs_1_), channel_id=1, source_target_pairs={{4,8},{8,4},{5,9},{9,5},{6,10},{10,6},{7,11},{11,7},{20,24},{24,20... | collective-permute-start | bytes 1228808 | tf_op jit(solution)/shard_map/cond/branch_0_fun/ppermute | solution.py:638
  45.0 22.9 %collective-permute-start.23 = (bf16[22,64,256]{2,1,0:T(8,128)(2,1)S(1)}, bf16[22,64,256]{2,1,0:T(8,128)(2,1)S(1)}, u32[]{:S(2)}, u32[]{:S(2)}) collective-permute-start(bf16[22,64,256]{2,1,0:T(8,128)(2,1)S(1)} %add.126), channel_id=1, source_target_pairs={{4,0},{8,12},{5,1},{9,13},{6,2},{10,14},{7,3},{11,15},{20,16},{24,... | collective-permute-start | bytes 2162696 | tf_op jit(solution)/shard_map/cond/branch_0_fun/ppermute | solution.py:638
  46.3 27.3 %collective-permute-start.24 = (bf16[25,64,128]{2,1,0:T(8,128)(2,1)S(1)}, bf16[25,64,128]{2,1,0:T(8,128)(2,1)S(1)}, u32[]{:S(2)}, u32[]{:S(2)}) collective-permute-start(bf16[25,64,128]{2,1,0:T(8,128)(2,1)S(1)} %collective-permute-done.22.refs_4_), channel_id=1, source_target_pairs={{4,0},{8,12},{5,1},{9,13},{6,2},{10,14},{7,3},{11,15},{20,16},{24,... | collective-permute-start | bytes 1228808 | tf_op jit(solution)/shard_map/cond/branch_0_fun/ppermute | solution.py:638
  80.2 16.5 %collective-permute-start.75 = (f32[2,128,128]{1,0,2:T(2,128)S(1)}, f32[2,128,128]{1,0,2:T(2,128)S(1)}, u32[]{:S(2)}, u32[]{:S(2)}) collective-permute-start(f32[2,128,128]{1,0,2:T(2,128)S(1)} %copy.17), channel_id=1, source_target_pairs={{0,3},{1,2},{2,1},{3,0},{4,7},{5,6},{6,5},{7,4},{8,11},{9,10},{10,... | collective-permute-start | bytes 393224 | tf_op jit(solution)/shard_map/ppermute | solution.py:711
  81.6 17.6 %collective-permute-start.74 = (f32[2,128,128]{1,0,2:T(2,128)S(1)}, f32[2,128,128]{1,0,2:T(2,128)S(1)}, u32[]{:S(2)}, u32[]{:S(2)}) collective-permute-start(f32[2,128,128]{1,0,2:T(2,128)S(1)} %copy.16), channel_id=1, source_target_pairs={{0,2},{1,3},{2,0},{3,1},{4,6},{5,7},{6,4},{7,5},{8,10},{9,11},{10,... | collective-permute-start | bytes 393224 | tf_op jit(solution)/shard_map/ppermute | solution.py:711
  93.7 5.4 %collective-permute-start.73 = (f32[2,128,128]{1,0,2:T(2,128)S(1)}, f32[2,128,128]{1,0,2:T(2,128)S(1)}, u32[]{:S(2)}, u32[]{:S(2)}) collective-permute-start(f32[2,128,128]{1,0,2:T(2,128)S(1)} %copy.14), channel_id=1, source_target_pairs={{0,1},{1,0},{2,3},{3,2},{4,5},{5,4},{6,7},{7,6},{8,9},{9,8},{10,11... | collective-permute-start | bytes 393224 | tf_op jit(solution)/shard_map/ppermute | solution.py:711
  99.1 7.6 %collective-permute-start.76 = (f32[2,128,128]{1,0,2:T(2,128)S(1)}, f32[2,128,128]{1,0,2:T(2,128)S(1)}, u32[]{:S(2)}, u32[]{:S(2)}) collective-permute-start(f32[2,128,128]{1,0,2:T(2,128)S(1)} %bitcast.50), channel_id=1, source_target_pairs={{0,8},{1,12},{2,0},{3,4},{4,9},{5,13},{6,1},{7,5},{8,10},{9,14},{1... | collective-permute-start | bytes 393224 | tf_op jit(solution)/shard_map/ppermute | solution.py:714
  100.0 11.2 %collective-permute-start.77 = (f32[2,128,128]{1,0,2:T(2,128)S(1)}, f32[2,128,128]{1,0,2:T(2,128)S(1)}, u32[]{:S(2)}, u32[]{:S(2)}) collective-permute-start(f32[2,128,128]{1,0,2:T(2,128)S(1)} %bitcast.51), channel_id=1, source_target_pairs={{0,0},{1,4},{2,8},{3,12},{4,1},{5,5},{6,9},{7,13},{8,2},{9,6},{10,... | collective-permute-start | bytes 393224 | tf_op jit(solution)/shard_map/ppermute | solution.py:713
